TPU v7x, 32 devices: a whole 2x2x4 slice. The times are simulated.
32 devices in a mesh: groups: 2 (over y), seq: 16 (over z, x, core).
Axes of the slice: x: 2, y: 2, z: 4, core: 2. Of those that a mesh axis runs over, the one named last changes fastest.
Arguments:
- tokens: bfloat16 [8192, 256], P(('groups', 'seq')), parts along dimension 0, may hold values from -6 to 6
- norm_gain: float32 [256], replicated, may hold values from 0.1 to 1.9
- in_weight: bfloat16 [256, 768], replicated, may hold values from -0.375 to 0.375
- short_filter: float32 [3, 768], replicated, may hold values from -3 to 3
- spectra: bfloat16 [2, 256, 32, 256], P(None, None, 'seq'), may hold values from -6 to 6
- skip_gain: float32 [256], replicated, may hold values from -1 to 1
- out_weight: bfloat16 [256, 256], replicated, may hold values from -0.375 to 0.375
- mlp_gain: float32 [256], replicated, may hold values from 0.1 to 1.9
- up_weight: bfloat16 [256, 1024], replicated, may hold values from -0.375 to 0.375
- down_weight: bfloat16 [1024, 256], replicated, may hold values from -0.1875 to 0.1875
Outputs:
- result: bfloat16 [8192, 256], P(('groups', 'seq')), parts along dimension 0
There are 2 independent parts, one for each index of `groups`. A program takes and returns all parts, laid end to end along the dimension named above; an argument that names none is the same for every part. Nothing has to cross between parts.
All inputs are finite; a program needn't handle non-finite values.
Results may differ from a plain program's by a relative error of at most 0.013.
Values may be sent and summed in bfloat16 or wider, within the bound.
A program may use at most 64 MiB of HBM per device.

v0:
```python
import math
import jax
import jax.numpy as jnp
from jax import lax
from jax.sharding import PartitionSpec as P

exact = lax.Precision.HIGHEST
epsilon = 1e-06


def passed_along(value, axis, steps):
    count = lax.axis_size(axis)
    first, last = (max(0, -steps), min(count, count - steps))
    return lax.ppermute(value, axis, [(source, source + steps) for source in range(first, last)])


def as_sent(array):
    return jax.tree.map(lambda a: a.astype(jnp.bfloat16) if a.dtype == jnp.float32 else a, array)


def rms_scale(values, gain):
    wide = values.astype(jnp.float32)
    return wide * lax.rsqrt(jnp.mean(wide * wide, axis=-1, keepdims=True) + epsilon) * gain


def phase_table(out_start, out_count, in_start, in_count, period):
    index_out = out_start + lax.iota(jnp.int32, out_count)[:, None]
    index_in = in_start + lax.iota(jnp.int32, in_count)[None, :]
    angle = 2.0 * math.pi / period * (index_out * index_in % period).astype(jnp.float32)
    return (jnp.cos(angle), jnp.sin(angle))


def apply_filter(spec_real, spec_imag, filt):
    filt_real = filt[0].astype(jnp.float32)
    filt_imag = filt[1].astype(jnp.float32)
    return (
        spec_real * filt_real - spec_imag * filt_imag,
        spec_real * filt_imag + spec_imag * filt_real,
    )


def rows_forward_first(piece, column_start, total):
    half = piece.shape[0]
    length = 2 * half
    count = piece.shape[1]
    cosine, sine = phase_table(0, length, 0, half, length)
    wide = piece.astype(jnp.float32)
    real_part = jnp.einsum("kn,nmc->kmc", cosine, wide, precision=exact)
    imag_part = -jnp.einsum("kn,nmc->kmc", sine, wide, precision=exact)
    turn_cos, turn_sin = phase_table(0, length, column_start, count, total)
    turn_cos = turn_cos[:, :, None]
    turn_sin = turn_sin[:, :, None]
    return (
        real_part * turn_cos + imag_part * turn_sin,
        imag_part * turn_cos - real_part * turn_sin,
    )


def rows_forward_second(parts):
    real_part, imag_part = parts
    size = real_part.shape[1]
    cosine, sine = phase_table(0, size, 0, size, size)
    real_cos = jnp.einsum("kn,anc->akc", cosine, real_part, precision=exact)
    real_sin = jnp.einsum("kn,anc->akc", sine, real_part, precision=exact)
    imag_cos = jnp.einsum("kn,anc->akc", cosine, imag_part, precision=exact)
    imag_sin = jnp.einsum("kn,anc->akc", sine, imag_part, precision=exact)
    return (real_cos + imag_sin, imag_cos - real_sin)


def rows_inverse_second(real_part, imag_part, row_start, total):
    rows = real_part.shape[0]
    size = real_part.shape[1]
    cosine, sine = phase_table(0, size, 0, size, size)
    real_cos = jnp.einsum("nk,akc->anc", cosine, real_part, precision=exact)
    real_sin = jnp.einsum("nk,akc->anc", sine, real_part, precision=exact)
    imag_cos = jnp.einsum("nk,akc->anc", cosine, imag_part, precision=exact)
    imag_sin = jnp.einsum("nk,akc->anc", sine, imag_part, precision=exact)
    out_real = real_cos - imag_sin
    out_imag = real_sin + imag_cos
    turn_cos, turn_sin = phase_table(row_start, rows, 0, size, total)
    turn_cos = turn_cos[:, :, None]
    turn_sin = turn_sin[:, :, None]
    return (out_real * turn_cos - out_imag * turn_sin, out_real * turn_sin + out_imag * turn_cos)


def rows_inverse_first(parts, total):
    real_part, imag_part = parts
    length = real_part.shape[0]
    half = length // 2
    cosine, sine = phase_table(0, half, 0, length, length)
    summed = jnp.einsum("nk,kmc->nmc", cosine, real_part, precision=exact) - jnp.einsum(
        "nk,kmc->nmc", sine, imag_part, precision=exact
    )
    return summed / total


def local(
    tokens,
    norm_gain,
    in_weight,
    short_filter,
    spectra,
    skip_gain,
    out_weight,
    mlp_gain,
    up_weight,
    down_weight,
):
    tok_rows, width = tokens.shape
    devices = lax.axis_size("seq")
    position = lax.axis_index("seq")
    total = 2 * tok_rows * devices
    inner = min(tok_rows, 512)
    outer = total // inner
    normed = rms_scale(tokens, norm_gain).astype(jnp.bfloat16)
    projected = jnp.dot(normed, in_weight, preferred_element_type=jnp.float32).astype(jnp.bfloat16)
    taps = short_filter.shape[0]
    earlier = passed_along(projected[tok_rows - (taps - 1) :], "seq", 1)
    extended = jnp.concatenate([earlier, projected], axis=0).astype(jnp.float32)
    mixed = short_filter[0] * extended[taps - 1 :]
    for lag in range(1, taps):
        mixed = mixed + short_filter[lag] * extended[taps - 1 - lag : taps - 1 - lag + tok_rows]
    query = mixed[:, :width].astype(jnp.bfloat16)
    driven = (mixed[:, width : 2 * width] * mixed[:, 2 * width :]).astype(jnp.bfloat16)
    local_cols = inner // devices
    col_start = position * local_cols
    blocked = driven.reshape(tok_rows // inner, inner, width)
    piece = lax.all_to_all(blocked, "seq", split_axis=1, concat_axis=0, tiled=True)
    real_part, imag_part = rows_forward_first(piece, col_start, total)
    spec_real, spec_imag = rows_forward_second(
        (
            lax.all_to_all(
                real_part.astype(jnp.bfloat16), "seq", split_axis=0, concat_axis=1, tiled=True
            ).astype(real_part.dtype),
            lax.all_to_all(
                imag_part.astype(jnp.bfloat16), "seq", split_axis=0, concat_axis=1, tiled=True
            ).astype(imag_part.dtype),
        )
    )
    resident = jnp.transpose(spectra, (0, 2, 3, 1))
    prod_real, prod_imag = apply_filter(spec_real, spec_imag, resident)
    local_rows = outer // devices
    back_real, back_imag = rows_inverse_second(prod_real, prod_imag, position * local_rows, total)
    response_cols = rows_inverse_first(
        (
            lax.all_to_all(
                as_sent(back_real), "seq", split_axis=1, concat_axis=0, tiled=True
            ).astype(back_real.dtype),
            lax.all_to_all(
                as_sent(back_imag), "seq", split_axis=1, concat_axis=0, tiled=True
            ).astype(back_imag.dtype),
        ),
        total,
    )
    response_cols = response_cols + skip_gain[None, None, :] * piece.astype(jnp.float32)
    response = lax.all_to_all(
        response_cols, "seq", split_axis=0, concat_axis=1, tiled=True
    ).reshape(tok_rows, width)
    gated = (query.astype(jnp.float32) * response).astype(jnp.bfloat16)
    hidden_state = (
        tokens.astype(jnp.float32) + jnp.dot(gated, out_weight, preferred_element_type=jnp.float32)
    ).astype(jnp.bfloat16)
    second_norm = rms_scale(hidden_state, mlp_gain).astype(jnp.bfloat16)
    activated = jax.nn.gelu(
        jnp.dot(second_norm, up_weight, preferred_element_type=jnp.float32), approximate=True
    ).astype(jnp.bfloat16)
    return (
        hidden_state.astype(jnp.float32)
        + jnp.dot(activated, down_weight, preferred_element_type=jnp.float32)
    ).astype(jnp.bfloat16)


def solution(mesh):
    in_specs = (
        P(("groups", "seq"), None),
        P(),
        P(),
        P(),
        P(None, None, "seq", None),
        P(),
        P(),
        P(),
        P(),
        P(),
    )
    out_specs = P(("groups", "seq"), None)
    return jax.shard_map(local, mesh=mesh, in_specs=in_specs, out_specs=out_specs, check_vma=False)
```

profile of v0, /device:TPU:0, one launch (start us, length us, event | category | flops | bytes accessed | tf_op | source)
XLA Modules:
  0.0 113.2 jit_solution(16862313538930423906)
XLA Ops:
  0.0 0.0 copy-start
  0.0 1.1 copy.59
  1.1 0.1 fusion.24
  1.1 0.0 copy-start.5
  1.2 0.0 copy-done.2
  1.2 0.6 copy-done.5
  1.8 0.4 convolution_convert_fusion
  2.2 2.4 %collective-permute-start = (bf16[2,768]{1,0:T(2,128)(2,1)S(1)}, bf16[2,768]{1,0:T(2,128)(2,1)S(1)}, u32[]{:S(2)}, u32[]{:S(2)}) collective-permute-start(bf16[2,768]{1,0:T(2,128)(2,1)S(1)} %slice.49), channel_id=1, source_target_pairs={{0,1},{1,2},{2,3},{3,4},{4,5},{5,6},{6,7},{7,8},{8,9},{9,10},{10,1... | collective-permute-start | bytes 9224 | tf_op jit(solution)/shard_map/ppermute | solution.py:14
  4.6 0.0 copy-done.4
  4.7 0.8 collective-permute-done
  5.4 0.1 maximum_convert_fusion
  5.5 0.2 fusion.15
  5.8 0.2 copy.98
  6.0 0.5 broadcast.303
  6.5 1.4 %reduce.6 = bf16[256,256]{1,0:T(8,128)(2,1)S(1)} reduce(bf16[256,1,256]{2,1,0:T(2,128)(2,1)S(1)} %bitcast.118, bf16[]{:T(256)} %broadcast.303), dimensions={1}, to_apply=%bitcast.110.reduce_sub_computation | reduce | bytes 262146
  7.9 0.7 reshape.163
  8.6 9.1 %all-to-all-start = ((bf16[16,2,2048]{2,1,0:T(2,128)(2,1)}), bf16[16,2,2048]{2,1,0:T(2,128)(2,1)S(1)}, u32[]{:S(2)}, u32[]{:S(2)}) async-start(bf16[16,2,2048]{2,1,0:T(2,128)(2,1)} %reshape.163), calls=%async_computation | async-start | bytes 262144 | tf_op jit(solution)/shard_map/all_to_all | solution.py:128
  17.7 0.1 fusion.101
  17.9 7.8 %all-to-all-done = bf16[16,2,2048]{2,1,0:T(2,128)(2,1)S(1)} async-done(((bf16[16,2,2048]{2,1,0:T(2,128)(2,1)}), bf16[16,2,2048]{2,1,0:T(2,128)(2,1)S(1)}, u32[]{:S(2)}, u32[]{:S(2)}) %all-to-all-start) | async-done | bytes 131104 | tf_op jit(solution)/shard_map/all_to_all | solution.py:128
  25.6 0.1 reshape.164
  25.8 0.5 fusion.69
  26.3 0.6 add_convert_fusion.1
  26.9 0.9 copy.63
  27.7 3.5 %all-to-all-start.1 = ((bf16[32,16,256]{2,1,0:T(8,128)(2,1)}), bf16[32,16,256]{2,1,0:T(8,128)(2,1)S(1)}, u32[]{:S(2)}, u32[]{:S(2)}) async-start(bf16[32,16,256]{2,1,0:T(8,128)(2,1)} %copy.63), calls=%async_computation.1 | async-start | bytes 524288 | tf_op jit(solution)/shard_map/all_to_all | solution.py:132
  31.3 0.0 copy-start.1
  31.3 0.8 copy.66
  32.1 9.2 %all-to-all-done.1 = bf16[32,16,256]{2,1,0:T(8,128)(2,1)S(1)} async-done(((bf16[32,16,256]{2,1,0:T(8,128)(2,1)}), bf16[32,16,256]{2,1,0:T(8,128)(2,1)S(1)}, u32[]{:S(2)}, u32[]{:S(2)}) %all-to-all-start.1) | async-done | bytes 262176 | tf_op jit(solution)/shard_map/all_to_all | solution.py:132
  41.3 3.7 %all-to-all-start.2 = ((bf16[32,16,256]{2,1,0:T(8,128)(2,1)}), bf16[32,16,256]{2,1,0:T(8,128)(2,1)S(1)}, u32[]{:S(2)}, u32[]{:S(2)}) async-start(bf16[32,16,256]{2,1,0:T(8,128)(2,1)} %copy.66), calls=%async_computation.2 | async-start | bytes 524288 | tf_op jit(solution)/shard_map/all_to_all | solution.py:135
  45.0 0.0 copy-done.1
  45.0 0.1 copy.97
  45.1 0.1 fusion.108
  45.3 9.6 %all-to-all-done.2 = bf16[32,16,256]{2,1,0:T(8,128)(2,1)S(1)} async-done(((bf16[32,16,256]{2,1,0:T(8,128)(2,1)}), bf16[32,16,256]{2,1,0:T(8,128)(2,1)S(1)}, u32[]{:S(2)}, u32[]{:S(2)}) %all-to-all-start.2) | async-done | bytes 262176 | tf_op jit(solution)/shard_map/all_to_all | solution.py:135
  54.8 1.4 %fusion.42 = f32[2,256,256]{2,1,0:T(8,128)S(1)} fusion(bf16[2,256,256]{2,1,0:T(8,128)(2,1)S(1)} %bitcast.126), kind=kOutput, calls=%fused_computation.74 | convolution fusion | flops 403570688 | bytes 786432 | tf_op jit(solution)/shard_map/kn,anc->akc/dot_general | solution.py:65
  56.3 1.4 %fusion.44 = f32[2,256,256]{2,1,0:T(8,128)S(1)} fusion(bf16[2,256,256]{2,1,0:T(8,128)(2,1)S(1)} %bitcast.124), kind=kOutput, calls=%fused_computation.76 | convolution fusion | flops 403570688 | bytes 786432 | tf_op jit(solution)/shard_map/kn,anc->akc/dot_general | solution.py:63
  57.7 1.4 %fusion = f32[2,256,256]{1,2,0:T(8,128)S(1)} fusion(f32[2,256,256]{2,1,0:T(8,128)S(1)} %fusion.42, bf16[2,256,256]{2,1,0:T(8,128)(2,1)S(1)} %bitcast.125), kind=kOutput, calls=%fused_computation.4 | convolution fusion | flops 403701760 | bytes 1310720 | tf_op jit(solution)/shard_map/kn,anc->akc/dot_general | solution.py:64
  59.1 1.4 %fusion.1 = f32[2,256,256]{1,2,0:T(8,128)S(1)} fusion(f32[2,256,256]{2,1,0:T(8,128)S(1)} %fusion.44, bf16[2,256,256]{2,1,0:T(8,128)(2,1)S(1)} %bitcast.127), kind=kOutput, calls=%fused_computation.6 | convolution fusion | flops 403701760 | bytes 1310720 | tf_op jit(solution)/shard_map/kn,anc->akc/dot_general | solution.py:66
  60.5 1.6 %fusion.34 = f32[2,256,256]{2,1,0:T(8,128)S(1)} fusion(f32[2,256,256]{1,2,0:T(8,128)S(1)} %fusion, f32[2,256,256]{1,2,0:T(8,128)S(1)} %fusion.1, bf16[2,2,256,256]{2,3,1,0:T(8,128)(2,1)S(1)} %bitcast.114), kind=kOutput, calls=%fused_computation.66 | convolution fusion | flops 404226048 | bytes 2097152 | tf_op jit(solution)/shard_map/nk,akc->anc/dot_general | solution.py:75
  62.1 1.6 %fusion.40 = f32[2,256,256]{2,1,0:T(8,128)S(1)} fusion(f32[2,256,256]{1,2,0:T(8,128)S(1)} %fusion, f32[2,256,256]{1,2,0:T(8,128)S(1)} %fusion.1, bf16[2,2,256,256]{2,3,1,0:T(8,128)(2,1)S(1)} %bitcast.115), kind=kOutput, calls=%fused_computation.72 | convolution fusion | flops 404226048 | bytes 2097152 | tf_op jit(solution)/shard_map/nk,akc->anc/dot_general | solution.py:74
  63.8 1.6 %convolution_add_fusion.1 = f32[2,256,256]{2,1,0:T(8,128)S(1)} fusion(f32[2,256,256]{2,1,0:T(8,128)S(1)} %fusion.34, f32[2,256,256]{1,2,0:T(8,128)S(1)} %fusion.1, f32[2,256,256]{1,2,0:T(8,128)S(1)} %fusion, bf16[2,2,256,256]{2,3,1,0:T(8,128)(2,1)S(1)} %bitcast.116), kind=kOutput, calls=%fused_computation.7 | convolution fusion | flops 404357120 | bytes 2621440 | tf_op jit(solution)/shard_map/nk,akc->anc/dot_general | solution.py:76
  65.4 1.9 %fusion.31 = (bf16[2,256,256]{1,2,0:T(8,128)(2,1)S(1)}, bf16[2,256,256]{1,2,0:T(8,128)(2,1)S(1)}) fusion(f32[2,256,256]{2,1,0:T(8,128)S(1)} %convolution_add_fusion.1, f32[2,256]{1,0:T(2,128)S(1)} %get-tuple-element.13, f32[2,256]{1,0:T(2,128)S(1)} %get-tuple-element.12, f32[2,256,256]{2,1,0:T(8,128)S(1)} %fusion.40, f32[2,256,256]{1,2,0:T(8,128)S(1)} %fusion.1, ...), kind=kOutput, calls=%fused_computation.58 | convolution fusion | flops 405405696 | bytes 3149824 | tf_op jit(solution)/shard_map/nk,akc->anc/dot_general | solution.py:77
  67.3 0.9 copy.75
  68.1 3.5 %all-to-all-start.4 = ((bf16[2,256,256]{2,0,1:T(2,128)(2,1)}), bf16[2,256,256]{2,0,1:T(2,128)(2,1)S(1)}, u32[]{:S(2)}, u32[]{:S(2)}) async-start(bf16[2,256,256]{2,0,1:T(2,128)(2,1)} %copy.75), calls=%async_computation.4 | async-start | bytes 524288 | tf_op jit(solution)/shard_map/all_to_all | solution.py:149
  71.7 0.9 copy.72
  72.5 9.1 %all-to-all-done.4 = bf16[2,256,256]{2,0,1:T(2,128)(2,1)S(1)} async-done(((bf16[2,256,256]{2,0,1:T(2,128)(2,1)}), bf16[2,256,256]{2,0,1:T(2,128)(2,1)S(1)}, u32[]{:S(2)}, u32[]{:S(2)}) %all-to-all-start.4) | async-done | bytes 262176 | tf_op jit(solution)/shard_map/all_to_all | solution.py:149
  81.7 3.5 %all-to-all-start.3 = ((bf16[2,256,256]{2,0,1:T(2,128)(2,1)}), bf16[2,256,256]{2,0,1:T(2,128)(2,1)S(1)}, u32[]{:S(2)}, u32[]{:S(2)}) async-start(bf16[2,256,256]{2,0,1:T(2,128)(2,1)} %copy.72), calls=%async_computation.3 | async-start | bytes 524288 | tf_op jit(solution)/shard_map/all_to_all | solution.py:146
  85.3 0.3 copy.77
  85.5 0.1 all_to_all.85
  85.7 9.6 %all-to-all-done.3 = bf16[2,256,256]{2,0,1:T(2,128)(2,1)S(1)} async-done(((bf16[2,256,256]{2,0,1:T(2,128)(2,1)}), bf16[2,256,256]{2,0,1:T(2,128)(2,1)S(1)}, u32[]{:S(2)}, u32[]{:S(2)}) %all-to-all-start.3) | async-done | bytes 262176 | tf_op jit(solution)/shard_map/all_to_all | solution.py:146
  95.3 0.3 copy.74
  95.5 0.1 all_to_all.81
  95.7 0.0 copy-start.6
  95.7 0.3 fusion.83
  96.0 0.4 copy-done.6
  96.3 0.3 fusion.3
  96.7 0.2 copy.79
  96.8 12.8 %all_to_all.93 = f32[16,16,256]{2,1,0:T(8,128)S(1)} all-to-all(f32[16,16,256]{2,1,0:T(8,128)S(1)} %copy.79), channel_id=1, replica_groups=mesh['groups'=2,'seq'=16] {'seq'}, dimensions={0} | all-to-all | bytes 524288 | tf_op jit(solution)/shard_map/all_to_all | solution.py:156
  109.7 0.9 copy-done.3
  110.6 0.3 multiply_reduce_fusion
  110.8 0.0 copy-start.8
  110.8 0.0 copy-done
  110.8 0.0 copy-done.7
  110.9 0.7 copy-done.8
  111.5 0.9 fusion.6
  112.4 0.8 copy.81
  (17 shorter events, 0.2 us)
Async XLA Ops:
  0.0 110.8 %copy-start = (bf16[1024,256]{1,0:T(8,128)(2,1)S(1)}, bf16[1024,256]{1,0:T(8,128)(2,1)}, u32[]{:S(2)}) copy-start(bf16[1024,256]{1,0:T(8,128)(2,1)} %param.19) | copy-start | bytes 1572868
  0.0 1.2 %copy-start.2 = (bf16[256,768]{1,0:T(8,128)(2,1)S(1)}, bf16[256,768]{1,0:T(8,128)(2,1)}, u32[]{:S(2)}) copy-start(bf16[256,768]{1,0:T(8,128)(2,1)} %param.12) | copy-start | bytes 1179652
  1.1 0.7 copy-start.5
  1.8 2.8 %copy-start.4 = (f32[3,768]{1,0:T(4,128)S(1)}, f32[3,768]{1,0:T(4,128)}, u32[]{:S(2)}) copy-start(f32[3,768]{1,0:T(4,128)} %param.13) | copy-start | bytes 27652
  2.2 3.2 %collective-permute-start = (bf16[2,768]{1,0:T(2,128)(2,1)S(1)}, bf16[2,768]{1,0:T(2,128)(2,1)S(1)}, u32[]{:S(2)}, u32[]{:S(2)}) collective-permute-start(bf16[2,768]{1,0:T(2,128)(2,1)S(1)} %slice.49), channel_id=1, source_target_pairs={{0,1},{1,2},{2,3},{3,4},{4,5},{5,6},{6,7},{7,8},{8,9},{9,10},{10,1... | collective-permute-start | bytes 9224 | tf_op jit(solution)/shard_map/ppermute | solution.py:14
  8.6 17.0 %all-to-all-start = ((bf16[16,2,2048]{2,1,0:T(2,128)(2,1)}), bf16[16,2,2048]{2,1,0:T(2,128)(2,1)S(1)}, u32[]{:S(2)}, u32[]{:S(2)}) async-start(bf16[16,2,2048]{2,1,0:T(2,128)(2,1)} %reshape.163), calls=%async_computation | async-start | bytes 262144 | tf_op jit(solution)/shard_map/all_to_all | solution.py:128
  27.7 13.5 %all-to-all-start.1 = ((bf16[32,16,256]{2,1,0:T(8,128)(2,1)}), bf16[32,16,256]{2,1,0:T(8,128)(2,1)S(1)}, u32[]{:S(2)}, u32[]{:S(2)}) async-start(bf16[32,16,256]{2,1,0:T(8,128)(2,1)} %copy.63), calls=%async_computation.1 | async-start | bytes 524288 | tf_op jit(solution)/shard_map/all_to_all | solution.py:132
  31.3 13.7 %copy-start.1 = (bf16[2,256,2,256]{3,2,1,0:T(2,128)(2,1)S(1)}, bf16[2,256,2,256]{3,2,1,0:T(2,128)(2,1)}, u32[]{:S(2)}) copy-start(bf16[2,256,2,256]{3,2,1,0:T(2,128)(2,1)} %param.14) | copy-start | bytes 1572868
  41.3 13.5 %all-to-all-start.2 = ((bf16[32,16,256]{2,1,0:T(8,128)(2,1)}), bf16[32,16,256]{2,1,0:T(8,128)(2,1)S(1)}, u32[]{:S(2)}, u32[]{:S(2)}) async-start(bf16[32,16,256]{2,1,0:T(8,128)(2,1)} %copy.66), calls=%async_computation.2 | async-start | bytes 524288 | tf_op jit(solution)/shard_map/all_to_all | solution.py:135
  68.1 13.5 %all-to-all-start.4 = ((bf16[2,256,256]{2,0,1:T(2,128)(2,1)}), bf16[2,256,256]{2,0,1:T(2,128)(2,1)S(1)}, u32[]{:S(2)}, u32[]{:S(2)}) async-start(bf16[2,256,256]{2,0,1:T(2,128)(2,1)} %copy.75), calls=%async_computation.4 | async-start | bytes 524288 | tf_op jit(solution)/shard_map/all_to_all | solution.py:149
  81.7 13.5 %all-to-all-start.3 = ((bf16[2,256,256]{2,0,1:T(2,128)(2,1)}), bf16[2,256,256]{2,0,1:T(2,128)(2,1)S(1)}, u32[]{:S(2)}, u32[]{:S(2)}) async-start(bf16[2,256,256]{2,0,1:T(2,128)(2,1)} %copy.72), calls=%async_computation.3 | async-start | bytes 524288 | tf_op jit(solution)/shard_map/all_to_all | solution.py:146
  95.7 0.7 copy-start.6
  109.6 0.9 copy-start.3
  109.7 1.2 %copy-start.7 = (bf16[256,1024]{1,0:T(8,128)(2,1)S(1)}, bf16[256,1024]{1,0:T(8,128)(2,1)}, u32[]{:S(2)}) copy-start(bf16[256,1024]{1,0:T(8,128)(2,1)} %param.18) | copy-start | bytes 1572868
  110.8 0.7 copy-start.8
where the time goes:
time: 114 us; the launch traced here: 113 us
  waiting for transfers between devices  46 us (40%)
  starting transfers between devices  25.8 us (23%)
  matrix products  15.6 us (14%)
  blocking collectives  12.8 us (11%)
  local copies, waits for them, and re-layouts  10.5 us (9%)
  other arithmetic  2.12 us (2%)
    all_to_all x1, blocking collectives, local(): lax.all_to_all(response_cols, 'seq', split_axis=0, concat_axis=1, tiled=T...  12.8 us
    all_to_all x1, waiting for transfers between devices, local(): lax.all_to_all(as_sent(back_real), 'seq', split_axis=1, concat_axis=0, ti...  9.58 us
    all_to_all x1, waiting for transfers between devices, local(): lax.all_to_all(imag_part.astype(jnp.bfloat16), 'seq', split_axis=0, conca...  9.56 us
    all_to_all x1, waiting for transfers between devices, local(): lax.all_to_all(real_part.astype(jnp.bfloat16), 'seq', split_axis=0, conca...  9.15 us
    all_to_all x1, waiting for transfers between devices, local(): lax.all_to_all(as_sent(back_imag), 'seq', split_axis=1, concat_axis=0, ti...  9.15 us
    all_to_all x1, starting transfers between devices, local(): lax.all_to_all(blocked, 'seq', split_axis=1, concat_axis=0, tiled=True)  9.1 us
    all_to_all x1, waiting for transfers between devices, local(): lax.all_to_all(blocked, 'seq', split_axis=1, concat_axis=0, tiled=True)  7.79 us
    unnamed x24, local copies, waits for them, and re-layouts  5.05 us
  transfers between devices with their start and end apart: 6, of which 6 were waited for; matrix products, arithmetic and copies ran while one was open for 2% of the time, Pallas kernels for 0%

commit v1 on v0

--- a/solution.py
+++ b/solution.py
@@ -6,6 +6,17 @@
 
 exact = lax.Precision.HIGHEST
 epsilon = 1e-06
+
+
+def _link_indices(body, dimension_no, unit):
+    part_now, res = (body.shape[:dimension_no], body.shape[dimension_no + 1 :])
+    return jnp.moveaxis(body.reshape(*part_now, unit, -1, *res), dimension_no, 0)
+
+
+def group_draw(matrix, axis_no):
+    field_out = list(matrix.shape[1:])
+    field_out[axis_no] *= matrix.shape[0]
+    return jnp.moveaxis(matrix, 0, axis_no).reshape(field_out)
 
 
 def passed_along(value, axis, steps):
@@ -106,6 +117,23 @@
     up_weight,
     down_weight,
 ):
+
+    def _solve_cubes(vec, row_axis, tile_in, u):
+        view_out, r2 = (lax.axis_size(row_axis), lax.axis_index(row_axis))
+        h_now = _link_indices(vec, tile_in, view_out)
+        history = [h_now[r2]]
+        for d in range(1, view_out):
+            a_now = h_now[(r2 + d) % view_out]
+            block_now = lax.ppermute(
+                a_now,
+                axis_name=row_axis,
+                perm=[(ix, (ix + d) % view_out) for ix in range(view_out)],
+            )
+            history.append(block_now)
+        found_now = jnp.stack(history)
+        h_now = found_now[(r2 - jnp.arange(view_out)) % view_out]
+        return group_draw(h_now, u)
+
     tok_rows, width = tokens.shape
     devices = lax.axis_size("seq")
     position = lax.axis_index("seq")
@@ -129,9 +157,7 @@
     real_part, imag_part = rows_forward_first(piece, col_start, total)
     spec_real, spec_imag = rows_forward_second(
         (
-            lax.all_to_all(
-                real_part.astype(jnp.bfloat16), "seq", split_axis=0, concat_axis=1, tiled=True
-            ).astype(real_part.dtype),
+            _solve_cubes(real_part.astype(jnp.bfloat16), "seq", 0, 1).astype(real_part.dtype),
             lax.all_to_all(
                 imag_part.astype(jnp.bfloat16), "seq", split_axis=0, concat_axis=1, tiled=True
             ).astype(imag_part.dtype),

time: 114 us -> 118 us (1.035)
  starting transfers between devices: 25.8 us -> 43.5 us
  waiting for transfers between devices: 46 us -> 31.7 us
    ppermute x0 -> x15, starting transfers between devices: none -> 16.6 us  [_solve_cubes(): lax.ppermute(a_now, axis_name=row_axis, perm=[(ix, (ix + d) % view_out) f...]
    all_to_all x1, waiting for transfers between devices: 9.56 us -> 0.01 us  [local(): lax.all_to_all(imag_part.astype(jnp.bfloat16), 'seq', split_axis=0, conca...]
    all_to_all x1 -> x0, waiting for transfers between devices: 9.15 us -> none  [local(): lax.all_to_all(real_part.astype(jnp.bfloat16), 'seq', split_axis=0, conca...]
    ppermute x0 -> x15, waiting for transfers between devices: none -> 4.91 us  [_solve_cubes(): lax.ppermute(a_now, axis_name=row_axis, perm=[(ix, (ix + d) % view_out) f...]
    all_to_all x1 -> x0, starting transfers between devices: 3.53 us -> none  [local(): lax.all_to_all(real_part.astype(jnp.bfloat16), 'seq', split_axis=0, conca...]
    all_to_all x1, starting transfers between devices: 3.71 us -> 6.1 us  [local(): lax.all_to_all(imag_part.astype(jnp.bfloat16), 'seq', split_axis=0, conca...]
    all_to_all x1, starting transfers between devices: 3.53 us -> 5.8 us  [local(): lax.all_to_all(as_sent(back_imag), 'seq', split_axis=1, concat_axis=0, ti...]
    unnamed x24 -> x39, local copies, waits for them, and re-layouts: 5.05 us -> 5.09 us
  transfers between devices with their start and end apart: 6 -> 20, of which waited for: 6 -> 7; matrix products, arithmetic and copies ran while one was open for 2% -> 4% of each run, Pallas kernels for 0% -> 0%
where the time goes in v1:
time: 118 us; the launch traced here: 117 us
  starting transfers between devices  43.5 us (37%)
  waiting for transfers between devices  31.7 us (27%)
  matrix products  15.6 us (13%)
  blocking collectives  12.8 us (11%)
  local copies, waits for them, and re-layouts  10.8 us (9%)
  other arithmetic  2.14 us (2%)
    ppermute x15, starting transfers between devices, _solve_cubes(): lax.ppermute(a_now, axis_name=row_axis, perm=[(ix, (ix + d) % view_out) f...  16.6 us
    all_to_all x1, blocking collectives, local(): lax.all_to_all(response_cols, 'seq', split_axis=0, concat_axis=1, tiled=T...  12.8 us
    all_to_all x1, waiting for transfers between devices, local(): lax.all_to_all(as_sent(back_real), 'seq', split_axis=1, concat_axis=0, ti...  9.58 us
    all_to_all x1, waiting for transfers between devices, local(): lax.all_to_all(as_sent(back_imag), 'seq', split_axis=1, concat_axis=0, ti...  9.18 us
    all_to_all x1, starting transfers between devices, local(): lax.all_to_all(blocked, 'seq', split_axis=1, concat_axis=0, tiled=True)  9.1 us
    all_to_all x1, waiting for transfers between devices, local(): lax.all_to_all(blocked, 'seq', split_axis=1, concat_axis=0, tiled=True)  7.42 us
    all_to_all x1, starting transfers between devices, local(): lax.all_to_all(imag_part.astype(jnp.bfloat16), 'seq', split_axis=0, conca...  6.1 us
    all_to_all x1, starting transfers between devices, local(): lax.all_to_all(as_sent(back_imag), 'seq', split_axis=1, concat_axis=0, ti...  5.8 us
  transfers between devices with their start and end apart: 20, of which 7 were waited for; matrix products, arithmetic and copies ran while one was open for 4% of the time, Pallas kernels for 0%

profile of v1, /device:TPU:0, one launch (start us, length us, event | category | flops | bytes accessed | tf_op | source)
XLA Modules:
  0.0 117.4 jit_solution(6668257180061920393)
XLA Ops:
  0.0 1.1 copy.108
  1.2 0.6 copy-done.5
  1.8 0.4 convolution_convert_fusion
  2.3 2.4 %collective-permute-start = (bf16[2,768]{1,0:T(2,128)(2,1)S(1)}, bf16[2,768]{1,0:T(2,128)(2,1)S(1)}, u32[]{:S(2)}, u32[]{:S(2)}) collective-permute-start(bf16[2,768]{1,0:T(2,128)(2,1)S(1)} %slice.51), channel_id=1, source_target_pairs={{0,1},{1,2},{2,3},{3,4},{4,5},{5,6},{6,7},{7,8},{8,9},{9,10},{10,1... | collective-permute-start | bytes 9224 | tf_op jit(solution)/shard_map/ppermute | solution.py:25
  4.7 0.1 fusion.120
  4.8 0.6 collective-permute-done
  5.5 0.2 fusion.15
  5.8 0.2 copy.194
  6.0 0.5 broadcast.387
  6.5 1.4 %reduce.6 = bf16[256,256]{1,0:T(8,128)(2,1)S(1)} reduce(bf16[256,1,256]{2,1,0:T(2,128)(2,1)S(1)} %bitcast.195, bf16[]{:T(256)} %broadcast.387), dimensions={1}, to_apply=%bitcast.187.reduce_sub_computation | reduce | bytes 262146
  7.9 0.7 reshape.228
  8.6 9.1 %all-to-all-start = ((bf16[16,2,2048]{2,1,0:T(2,128)(2,1)}), bf16[16,2,2048]{2,1,0:T(2,128)(2,1)S(1)}, u32[]{:S(2)}, u32[]{:S(2)}) async-start(bf16[16,2,2048]{2,1,0:T(2,128)(2,1)} %reshape.228), calls=%async_computation | async-start | bytes 262144 | tf_op jit(solution)/shard_map/all_to_all | solution.py:156
  18.1 0.1 fusion.101
  18.3 7.4 %all-to-all-done = bf16[16,2,2048]{2,1,0:T(2,128)(2,1)S(1)} async-done(((bf16[16,2,2048]{2,1,0:T(2,128)(2,1)}), bf16[16,2,2048]{2,1,0:T(2,128)(2,1)S(1)}, u32[]{:S(2)}, u32[]{:S(2)}) %all-to-all-start) | async-done | bytes 131104 | tf_op jit(solution)/shard_map/all_to_all | solution.py:156
  25.7 0.1 reshape.229
  25.8 0.5 fusion.69
  26.3 0.6 add_convert_fusion.1
  26.9 0.1 reshape.206
  27.0 0.3 constant_dynamic-slice_fusion
  27.5 1.1 collective-permute-start.3
  28.7 1.0 collective-permute-start.4
  29.7 0.3 collective-permute-start.5
  30.0 0.8 copy.130
  30.9 6.1 %all-to-all-start.1 = ((bf16[32,16,256]{2,1,0:T(8,128)(2,1)}), bf16[32,16,256]{2,1,0:T(8,128)(2,1)S(1)}, u32[]{:S(2)}, u32[]{:S(2)}) async-start(bf16[32,16,256]{2,1,0:T(8,128)(2,1)} %copy.130), calls=%async_computation.1 | async-start | bytes 524288 | tf_op jit(solution)/shard_map/all_to_all | solution.py:161
  37.0 2.9 %collective-permute-start.6 = (bf16[2,16,256]{2,1,0:T(8,128)(2,1)S(1)}, bf16[2,16,256]{2,1,0:T(8,128)(2,1)S(1)}, u32[]{:S(2)}, u32[]{:S(2)}) collective-permute-start(bf16[2,16,256]{2,1,0:T(8,128)(2,1)S(1)} %bitcast.218), channel_id=1, source_target_pairs={{0,6},{1,7},{2,8},{3,9},{4,10},{5,11},{6,12},{7,13},{8,14},{9,15},... | collective-permute-start | bytes 49160 | tf_op jit(solution)/shard_map/ppermute | solution.py:127
  39.9 1.8 %collective-permute-start.7 = (bf16[2,16,256]{2,1,0:T(8,128)(2,1)S(1)}, bf16[2,16,256]{2,1,0:T(8,128)(2,1)S(1)}, u32[]{:S(2)}, u32[]{:S(2)}) collective-permute-start(bf16[2,16,256]{2,1,0:T(8,128)(2,1)S(1)} %bitcast.216), channel_id=1, source_target_pairs={{0,7},{1,8},{2,9},{3,10},{4,11},{5,12},{6,13},{7,14},{8,15},{9,0},... | collective-permute-start | bytes 49160 | tf_op jit(solution)/shard_map/ppermute | solution.py:127
  41.7 0.6 collective-permute-start.8
  42.4 2.3 %collective-permute-start.9 = (bf16[2,16,256]{2,1,0:T(8,128)(2,1)S(1)}, bf16[2,16,256]{2,1,0:T(8,128)(2,1)S(1)}, u32[]{:S(2)}, u32[]{:S(2)}) collective-permute-start(bf16[2,16,256]{2,1,0:T(8,128)(2,1)S(1)} %bitcast.212), channel_id=1, source_target_pairs={{0,9},{1,10},{2,11},{3,12},{4,13},{5,14},{6,15},{7,0},{8,1},{9,2},... | collective-permute-start | bytes 49160 | tf_op jit(solution)/shard_map/ppermute | solution.py:127
  44.6 1.5 %collective-permute-start.10 = (bf16[2,16,256]{2,1,0:T(8,128)(2,1)S(1)}, bf16[2,16,256]{2,1,0:T(8,128)(2,1)S(1)}, u32[]{:S(2)}, u32[]{:S(2)}) collective-permute-start(bf16[2,16,256]{2,1,0:T(8,128)(2,1)S(1)} %bitcast.210), channel_id=1, source_target_pairs={{0,10},{1,11},{2,12},{3,13},{4,14},{5,15},{6,0},{7,1},{8,2},{9,3},... | collective-permute-start | bytes 49160 | tf_op jit(solution)/shard_map/ppermute | solution.py:127
  46.1 3.5 %collective-permute-done.6 = bf16[2,16,256]{2,1,0:T(8,128)(2,1)S(1)} collective-permute-done((bf16[2,16,256]{2,1,0:T(8,128)(2,1)S(1)}, bf16[2,16,256]{2,1,0:T(8,128)(2,1)S(1)}, u32[]{:S(2)}, u32[]{:S(2)}) %collective-permute-start.6) | collective-permute-done | bytes 16416 | tf_op jit(solution)/shard_map/ppermute | solution.py:127
  49.6 1.5 %collective-permute-start.12 = (bf16[2,16,256]{2,1,0:T(8,128)(2,1)S(1)}, bf16[2,16,256]{2,1,0:T(8,128)(2,1)S(1)}, u32[]{:S(2)}, u32[]{:S(2)}) collective-permute-start(bf16[2,16,256]{2,1,0:T(8,128)(2,1)S(1)} %bitcast.208), channel_id=1, source_target_pairs={{0,12},{1,13},{2,14},{3,15},{4,0},{5,1},{6,2},{7,3},{8,4},{9,5},{1... | collective-permute-start | bytes 49160 | tf_op jit(solution)/shard_map/ppermute | solution.py:127
  51.1 1.0 collective-permute-start.14
  52.2 2.5 %collective-permute-start.15 = (bf16[2,16,256]{2,1,0:T(8,128)(2,1)S(1)}, bf16[2,16,256]{2,1,0:T(8,128)(2,1)S(1)}, u32[]{:S(2)}, u32[]{:S(2)}) collective-permute-start(bf16[2,16,256]{2,1,0:T(8,128)(2,1)S(1)} %bitcast.205), channel_id=1, source_target_pairs={{0,15},{1,0},{2,1},{3,2},{4,3},{5,4},{6,5},{7,6},{8,7},{9,8},{10,9... | collective-permute-start | bytes 49160 | tf_op jit(solution)/shard_map/ppermute | solution.py:127
  54.7 0.2 collective-permute-done.14
  54.9 1.2 %collective-permute-done.15 = bf16[2,16,256]{2,1,0:T(8,128)(2,1)S(1)} collective-permute-done((bf16[2,16,256]{2,1,0:T(8,128)(2,1)S(1)}, bf16[2,16,256]{2,1,0:T(8,128)(2,1)S(1)}, u32[]{:S(2)}, u32[]{:S(2)}) %collective-permute-start.15) | collective-permute-done | bytes 16416 | tf_op jit(solution)/shard_map/ppermute | solution.py:127
  56.1 0.6 gather_fusion
  56.7 1.4 %fusion.44 = f32[2,256,256]{2,1,0:T(8,128)S(1)} fusion(bf16[2,256,256]{2,1,0:T(8,128)(2,1)S(1)} %bitcast.201), kind=kOutput, calls=%fused_computation.77 | convolution fusion | flops 403570688 | bytes 786432 | tf_op jit(solution)/shard_map/kn,anc->akc/dot_general | solution.py:74
  58.2 1.4 %fusion.42 = f32[2,256,256]{2,1,0:T(8,128)S(1)} fusion(bf16[2,256,256]{2,1,0:T(8,128)(2,1)S(1)} %bitcast.203), kind=kOutput, calls=%fused_computation.75 | convolution fusion | flops 403570688 | bytes 786432 | tf_op jit(solution)/shard_map/kn,anc->akc/dot_general | solution.py:76
  59.6 1.4 %fusion = f32[2,256,256]{1,2,0:T(8,128)S(1)} fusion(f32[2,256,256]{2,1,0:T(8,128)S(1)} %fusion.42, bf16[2,256,256]{2,1,0:T(8,128)(2,1)S(1)} %bitcast.202), kind=kOutput, calls=%fused_computation.5 | convolution fusion | flops 403701760 | bytes 1310720 | tf_op jit(solution)/shard_map/kn,anc->akc/dot_general | solution.py:75
  61.0 1.4 %fusion.1 = f32[2,256,256]{1,2,0:T(8,128)S(1)} fusion(f32[2,256,256]{2,1,0:T(8,128)S(1)} %fusion.44, bf16[2,256,256]{2,1,0:T(8,128)(2,1)S(1)} %bitcast.204), kind=kOutput, calls=%fused_computation.7 | convolution fusion | flops 403701760 | bytes 1310720 | tf_op jit(solution)/shard_map/kn,anc->akc/dot_general | solution.py:77
  62.4 1.6 %fusion.34 = f32[2,256,256]{2,1,0:T(8,128)S(1)} fusion(f32[2,256,256]{1,2,0:T(8,128)S(1)} %fusion, f32[2,256,256]{1,2,0:T(8,128)S(1)} %fusion.1, bf16[2,2,256,256]{2,3,1,0:T(8,128)(2,1)S(1)} %bitcast.191), kind=kOutput, calls=%fused_computation.67 | convolution fusion | flops 404226048 | bytes 2097152 | tf_op jit(solution)/shard_map/nk,akc->anc/dot_general | solution.py:86
  64.1 1.6 %fusion.40 = f32[2,256,256]{2,1,0:T(8,128)S(1)} fusion(f32[2,256,256]{1,2,0:T(8,128)S(1)} %fusion, f32[2,256,256]{1,2,0:T(8,128)S(1)} %fusion.1, bf16[2,2,256,256]{2,3,1,0:T(8,128)(2,1)S(1)} %bitcast.192), kind=kOutput, calls=%fused_computation.73 | convolution fusion | flops 404226048 | bytes 2097152 | tf_op jit(solution)/shard_map/nk,akc->anc/dot_general | solution.py:85
  65.7 1.6 %convolution_add_fusion.1 = f32[2,256,256]{2,1,0:T(8,128)S(1)} fusion(f32[2,256,256]{2,1,0:T(8,128)S(1)} %fusion.34, f32[2,256,256]{1,2,0:T(8,128)S(1)} %fusion.1, f32[2,256,256]{1,2,0:T(8,128)S(1)} %fusion, bf16[2,2,256,256]{2,3,1,0:T(8,128)(2,1)S(1)} %bitcast.193), kind=kOutput, calls=%fused_computation.8 | convolution fusion | flops 404357120 | bytes 2621440 | tf_op jit(solution)/shard_map/nk,akc->anc/dot_general | solution.py:87
  67.3 1.9 %fusion.31 = (bf16[2,256,256]{1,2,0:T(8,128)(2,1)S(1)}, bf16[2,256,256]{1,2,0:T(8,128)(2,1)S(1)}) fusion(f32[2,256,256]{2,1,0:T(8,128)S(1)} %convolution_add_fusion.1, f32[2,256]{1,0:T(2,128)S(1)} %get-tuple-element.29, f32[2,256]{1,0:T(2,128)S(1)} %get-tuple-element.28, f32[2,256,256]{2,1,0:T(8,128)S(1)} %fusion.40, f32[2,256,256]{1,2,0:T(8,128)S(1)} %fusion.1, ...), kind=kOutput, calls=%fused_computation.59 | convolution fusion | flops 405405696 | bytes 3149824 | tf_op jit(solution)/shard_map/nk,akc->anc/dot_general | solution.py:88
  69.2 0.9 copy.139
  70.1 5.8 %all-to-all-start.3 = ((bf16[2,256,256]{2,0,1:T(2,128)(2,1)}), bf16[2,256,256]{2,0,1:T(2,128)(2,1)S(1)}, u32[]{:S(2)}, u32[]{:S(2)}) async-start(bf16[2,256,256]{2,0,1:T(2,128)(2,1)} %copy.139), calls=%async_computation.3 | async-start | bytes 524288 | tf_op jit(solution)/shard_map/all_to_all | solution.py:175
  75.9 0.9 copy.136
  76.7 9.2 %all-to-all-done.3 = bf16[2,256,256]{2,0,1:T(2,128)(2,1)S(1)} async-done(((bf16[2,256,256]{2,0,1:T(2,128)(2,1)}), bf16[2,256,256]{2,0,1:T(2,128)(2,1)S(1)}, u32[]{:S(2)}, u32[]{:S(2)}) %all-to-all-start.3) | async-done | bytes 262176 | tf_op jit(solution)/shard_map/all_to_all | solution.py:175
  85.9 3.5 %all-to-all-start.2 = ((bf16[2,256,256]{2,0,1:T(2,128)(2,1)}), bf16[2,256,256]{2,0,1:T(2,128)(2,1)S(1)}, u32[]{:S(2)}, u32[]{:S(2)}) async-start(bf16[2,256,256]{2,0,1:T(2,128)(2,1)} %copy.136), calls=%async_computation.2 | async-start | bytes 524288 | tf_op jit(solution)/shard_map/all_to_all | solution.py:172
  89.5 0.3 copy.141
  89.8 0.1 all_to_all.68
  89.9 9.6 %all-to-all-done.2 = bf16[2,256,256]{2,0,1:T(2,128)(2,1)S(1)} async-done(((bf16[2,256,256]{2,0,1:T(2,128)(2,1)}), bf16[2,256,256]{2,0,1:T(2,128)(2,1)S(1)}, u32[]{:S(2)}, u32[]{:S(2)}) %all-to-all-start.2) | async-done | bytes 262176 | tf_op jit(solution)/shard_map/all_to_all | solution.py:172
  99.5 0.3 copy.138
  99.8 0.1 all_to_all.64
  99.9 0.3 fusion.83
  100.2 0.4 copy-done.6
  100.6 0.3 fusion.3
  100.9 0.2 copy.143
  101.0 12.8 %all_to_all.75 = f32[16,16,256]{2,1,0:T(8,128)S(1)} all-to-all(f32[16,16,256]{2,1,0:T(8,128)S(1)} %copy.143), channel_id=1, replica_groups=mesh['groups'=2,'seq'=16] {'seq'}, dimensions={0} | all-to-all | bytes 524288 | tf_op jit(solution)/shard_map/all_to_all | solution.py:182
  113.9 0.9 copy-done.3
  114.8 0.3 multiply_reduce_fusion
  115.1 0.7 copy-done.8
  115.7 0.9 fusion.6
  116.6 0.8 copy.145
  (80 shorter events, 0.8 us)
Async XLA Ops:
  0.0 115.1 %copy-start = (bf16[1024,256]{1,0:T(8,128)(2,1)S(1)}, bf16[1024,256]{1,0:T(8,128)(2,1)}, u32[]{:S(2)}) copy-start(bf16[1024,256]{1,0:T(8,128)(2,1)} %param.19) | copy-start | bytes 1572868
  0.0 1.2 copy-start.2
  1.1 0.7 copy-start.5
  2.2 2.6 %copy-start.4 = (f32[3,768]{1,0:T(4,128)S(1)}, f32[3,768]{1,0:T(4,128)}, u32[]{:S(2)}) copy-start(f32[3,768]{1,0:T(4,128)} %param.13) | copy-start | bytes 27652
  2.3 3.2 %collective-permute-start = (bf16[2,768]{1,0:T(2,128)(2,1)S(1)}, bf16[2,768]{1,0:T(2,128)(2,1)S(1)}, u32[]{:S(2)}, u32[]{:S(2)}) collective-permute-start(bf16[2,768]{1,0:T(2,128)(2,1)S(1)} %slice.51), channel_id=1, source_target_pairs={{0,1},{1,2},{2,3},{3,4},{4,5},{5,6},{6,7},{7,8},{8,9},{9,10},{10,1... | collective-permute-start | bytes 9224 | tf_op jit(solution)/shard_map/ppermute | solution.py:25
  7.9 10.0 %copy-start.1 = (bf16[2,256,2,256]{3,2,1,0:T(2,128)(2,1)S(1)}, bf16[2,256,2,256]{3,2,1,0:T(2,128)(2,1)}, u32[]{:S(2)}) copy-start(bf16[2,256,2,256]{3,2,1,0:T(2,128)(2,1)} %param.14) | copy-start | bytes 1572868
  8.6 17.0 %all-to-all-start = ((bf16[16,2,2048]{2,1,0:T(2,128)(2,1)}), bf16[16,2,2048]{2,1,0:T(2,128)(2,1)S(1)}, u32[]{:S(2)}, u32[]{:S(2)}) async-start(bf16[16,2,2048]{2,1,0:T(2,128)(2,1)} %reshape.228), calls=%async_computation | async-start | bytes 262144 | tf_op jit(solution)/shard_map/all_to_all | solution.py:156
  27.4 9.6 %collective-permute-start.1 = (bf16[2,16,256]{2,1,0:T(8,128)(2,1)S(1)}, bf16[2,16,256]{2,1,0:T(8,128)(2,1)S(1)}, u32[]{:S(2)}, u32[]{:S(2)}) collective-permute-start(bf16[2,16,256]{2,1,0:T(8,128)(2,1)S(1)} %bitcast.219), channel_id=1, source_target_pairs={{0,1},{1,2},{2,3},{3,4},{4,5},{5,6},{6,7},{7,8},{8,9},{9,10},{10,1... | collective-permute-start | bytes 49160 | tf_op jit(solution)/shard_map/ppermute | solution.py:127
  27.5 12.4 %collective-permute-start.2 = (bf16[2,16,256]{2,1,0:T(8,128)(2,1)S(1)}, bf16[2,16,256]{2,1,0:T(8,128)(2,1)S(1)}, u32[]{:S(2)}, u32[]{:S(2)}) collective-permute-start(bf16[2,16,256]{2,1,0:T(8,128)(2,1)S(1)} %bitcast.217), channel_id=1, source_target_pairs={{0,2},{1,3},{2,4},{3,5},{4,6},{5,7},{6,8},{7,9},{8,10},{9,11},{10,... | collective-permute-start | bytes 49160 | tf_op jit(solution)/shard_map/ppermute | solution.py:127
  27.5 14.2 %collective-permute-start.3 = (bf16[2,16,256]{2,1,0:T(8,128)(2,1)S(1)}, bf16[2,16,256]{2,1,0:T(8,128)(2,1)S(1)}, u32[]{:S(2)}, u32[]{:S(2)}) collective-permute-start(bf16[2,16,256]{2,1,0:T(8,128)(2,1)S(1)} %bitcast.215), channel_id=1, source_target_pairs={{0,3},{1,4},{2,5},{3,6},{4,7},{5,8},{6,9},{7,10},{8,11},{9,12},{10... | collective-permute-start | bytes 49160 | tf_op jit(solution)/shard_map/ppermute | solution.py:127
  28.7 13.7 %collective-permute-start.4 = (bf16[2,16,256]{2,1,0:T(8,128)(2,1)S(1)}, bf16[2,16,256]{2,1,0:T(8,128)(2,1)S(1)}, u32[]{:S(2)}, u32[]{:S(2)}) collective-permute-start(bf16[2,16,256]{2,1,0:T(8,128)(2,1)S(1)} %bitcast.213), channel_id=1, source_target_pairs={{0,4},{1,5},{2,6},{3,7},{4,8},{5,9},{6,10},{7,11},{8,12},{9,13},{1... | collective-permute-start | bytes 49160 | tf_op jit(solution)/shard_map/ppermute | solution.py:127
  29.7 15.0 %collective-permute-start.5 = (bf16[2,16,256]{2,1,0:T(8,128)(2,1)S(1)}, bf16[2,16,256]{2,1,0:T(8,128)(2,1)S(1)}, u32[]{:S(2)}, u32[]{:S(2)}) collective-permute-start(bf16[2,16,256]{2,1,0:T(8,128)(2,1)S(1)} %bitcast.211), channel_id=1, source_target_pairs={{0,5},{1,6},{2,7},{3,8},{4,9},{5,10},{6,11},{7,12},{8,13},{9,14},{... | collective-permute-start | bytes 49160 | tf_op jit(solution)/shard_map/ppermute | solution.py:127
  30.9 27.3 %all-to-all-start.1 = ((bf16[32,16,256]{2,1,0:T(8,128)(2,1)}), bf16[32,16,256]{2,1,0:T(8,128)(2,1)S(1)}, u32[]{:S(2)}, u32[]{:S(2)}) async-start(bf16[32,16,256]{2,1,0:T(8,128)(2,1)} %copy.130), calls=%async_computation.1 | async-start | bytes 524288 | tf_op jit(solution)/shard_map/all_to_all | solution.py:161
  37.0 12.6 %collective-permute-start.6 = (bf16[2,16,256]{2,1,0:T(8,128)(2,1)S(1)}, bf16[2,16,256]{2,1,0:T(8,128)(2,1)S(1)}, u32[]{:S(2)}, u32[]{:S(2)}) collective-permute-start(bf16[2,16,256]{2,1,0:T(8,128)(2,1)S(1)} %bitcast.218), channel_id=1, source_target_pairs={{0,6},{1,7},{2,8},{3,9},{4,10},{5,11},{6,12},{7,13},{8,14},{9,15},... | collective-permute-start | bytes 49160 | tf_op jit(solution)/shard_map/ppermute | solution.py:127
  39.9 9.7 %collective-permute-start.7 = (bf16[2,16,256]{2,1,0:T(8,128)(2,1)S(1)}, bf16[2,16,256]{2,1,0:T(8,128)(2,1)S(1)}, u32[]{:S(2)}, u32[]{:S(2)}) collective-permute-start(bf16[2,16,256]{2,1,0:T(8,128)(2,1)S(1)} %bitcast.216), channel_id=1, source_target_pairs={{0,7},{1,8},{2,9},{3,10},{4,11},{5,12},{6,13},{7,14},{8,15},{9,0},... | collective-permute-start | bytes 49160 | tf_op jit(solution)/shard_map/ppermute | solution.py:127
  41.7 9.4 %collective-permute-start.8 = (bf16[2,16,256]{2,1,0:T(8,128)(2,1)S(1)}, bf16[2,16,256]{2,1,0:T(8,128)(2,1)S(1)}, u32[]{:S(2)}, u32[]{:S(2)}) collective-permute-start(bf16[2,16,256]{2,1,0:T(8,128)(2,1)S(1)} %bitcast.214), channel_id=1, source_target_pairs={{0,8},{1,9},{2,10},{3,11},{4,12},{5,13},{6,14},{7,15},{8,0},{9,1},... | collective-permute-start | bytes 49160 | tf_op jit(solution)/shard_map/ppermute | solution.py:127
  42.4 8.8 %collective-permute-start.9 = (bf16[2,16,256]{2,1,0:T(8,128)(2,1)S(1)}, bf16[2,16,256]{2,1,0:T(8,128)(2,1)S(1)}, u32[]{:S(2)}, u32[]{:S(2)}) collective-permute-start(bf16[2,16,256]{2,1,0:T(8,128)(2,1)S(1)} %bitcast.212), channel_id=1, source_target_pairs={{0,9},{1,10},{2,11},{3,12},{4,13},{5,14},{6,15},{7,0},{8,1},{9,2},... | collective-permute-start | bytes 49160 | tf_op jit(solution)/shard_map/ppermute | solution.py:127
  44.6 7.5 %collective-permute-start.10 = (bf16[2,16,256]{2,1,0:T(8,128)(2,1)S(1)}, bf16[2,16,256]{2,1,0:T(8,128)(2,1)S(1)}, u32[]{:S(2)}, u32[]{:S(2)}) collective-permute-start(bf16[2,16,256]{2,1,0:T(8,128)(2,1)S(1)} %bitcast.210), channel_id=1, source_target_pairs={{0,10},{1,11},{2,12},{3,13},{4,14},{5,15},{6,0},{7,1},{8,2},{9,3},... | collective-permute-start | bytes 49160 | tf_op jit(solution)/shard_map/ppermute | solution.py:127
  49.6 5.1 %collective-permute-start.11 = (bf16[2,16,256]{2,1,0:T(8,128)(2,1)S(1)}, bf16[2,16,256]{2,1,0:T(8,128)(2,1)S(1)}, u32[]{:S(2)}, u32[]{:S(2)}) collective-permute-start(bf16[2,16,256]{2,1,0:T(8,128)(2,1)S(1)} %bitcast.209), channel_id=1, source_target_pairs={{0,11},{1,12},{2,13},{3,14},{4,15},{5,0},{6,1},{7,2},{8,3},{9,4},{... | collective-permute-start | bytes 49160 | tf_op jit(solution)/shard_map/ppermute | solution.py:127
  49.6 5.1 %collective-permute-start.12 = (bf16[2,16,256]{2,1,0:T(8,128)(2,1)S(1)}, bf16[2,16,256]{2,1,0:T(8,128)(2,1)S(1)}, u32[]{:S(2)}, u32[]{:S(2)}) collective-permute-start(bf16[2,16,256]{2,1,0:T(8,128)(2,1)S(1)} %bitcast.208), channel_id=1, source_target_pairs={{0,12},{1,13},{2,14},{3,15},{4,0},{5,1},{6,2},{7,3},{8,4},{9,5},{1... | collective-permute-start | bytes 49160 | tf_op jit(solution)/shard_map/ppermute | solution.py:127
  51.1 3.6 %collective-permute-start.13 = (bf16[2,16,256]{2,1,0:T(8,128)(2,1)S(1)}, bf16[2,16,256]{2,1,0:T(8,128)(2,1)S(1)}, u32[]{:S(2)}, u32[]{:S(2)}) collective-permute-start(bf16[2,16,256]{2,1,0:T(8,128)(2,1)S(1)} %bitcast.207), channel_id=1, source_target_pairs={{0,13},{1,14},{2,15},{3,0},{4,1},{5,2},{6,3},{7,4},{8,5},{9,6},{10... | collective-permute-start | bytes 49160 | tf_op jit(solution)/shard_map/ppermute | solution.py:127
  51.1 3.8 %collective-permute-start.14 = (bf16[2,16,256]{2,1,0:T(8,128)(2,1)S(1)}, bf16[2,16,256]{2,1,0:T(8,128)(2,1)S(1)}, u32[]{:S(2)}, u32[]{:S(2)}) collective-permute-start(bf16[2,16,256]{2,1,0:T(8,128)(2,1)S(1)} %bitcast.206), channel_id=1, source_target_pairs={{0,14},{1,15},{2,0},{3,1},{4,2},{5,3},{6,4},{7,5},{8,6},{9,7},{10,... | collective-permute-start | bytes 49160 | tf_op jit(solution)/shard_map/ppermute | solution.py:127
  52.2 4.0 %collective-permute-start.15 = (bf16[2,16,256]{2,1,0:T(8,128)(2,1)S(1)}, bf16[2,16,256]{2,1,0:T(8,128)(2,1)S(1)}, u32[]{:S(2)}, u32[]{:S(2)}) collective-permute-start(bf16[2,16,256]{2,1,0:T(8,128)(2,1)S(1)} %bitcast.205), channel_id=1, source_target_pairs={{0,15},{1,0},{2,1},{3,2},{4,3},{5,4},{6,5},{7,6},{8,7},{9,8},{10,9... | collective-permute-start | bytes 49160 | tf_op jit(solution)/shard_map/ppermute | solution.py:127
  70.1 15.9 %all-to-all-start.3 = ((bf16[2,256,256]{2,0,1:T(2,128)(2,1)}), bf16[2,256,256]{2,0,1:T(2,128)(2,1)S(1)}, u32[]{:S(2)}, u32[]{:S(2)}) async-start(bf16[2,256,256]{2,0,1:T(2,128)(2,1)} %copy.139), calls=%async_computation.3 | async-start | bytes 524288 | tf_op jit(solution)/shard_map/all_to_all | solution.py:175
  85.9 13.5 %all-to-all-start.2 = ((bf16[2,256,256]{2,0,1:T(2,128)(2,1)}), bf16[2,256,256]{2,0,1:T(2,128)(2,1)S(1)}, u32[]{:S(2)}, u32[]{:S(2)}) async-start(bf16[2,256,256]{2,0,1:T(2,128)(2,1)} %copy.136), calls=%async_computation.2 | async-start | bytes 524288 | tf_op jit(solution)/shard_map/all_to_all | solution.py:172
  99.9 0.7 copy-start.6
  113.9 0.9 copy-start.3
  113.9 1.2 %copy-start.7 = (bf16[256,1024]{1,0:T(8,128)(2,1)S(1)}, bf16[256,1024]{1,0:T(8,128)(2,1)}, u32[]{:S(2)}) copy-start(bf16[256,1024]{1,0:T(8,128)(2,1)} %param.18) | copy-start | bytes 1572868
  115.0 0.7 copy-start.8
